TPU v7x, 32 devices: a whole 2x2x4 slice. The times are simulated.
32 devices in a mesh: seq: 4 (over y, x), grp: 8 (over z, core).
Axes of the slice: x: 2, y: 2, z: 4, core: 2. Of those that a mesh axis runs over, the one named last changes fastest.
Arguments:
- tokens: bfloat16 [8, 4608, 512], P('grp', 'seq'), may hold values from -6 to 6
- cotangent: bfloat16 [8, 4608, 512], P('grp', 'seq'), may hold values from -6 to 6
- lengths: int32 [8], P('grp'), may hold values from 3457 to 4608, as said below
- weight_query: float32 [512, 512], P(('seq', 'grp')), may hold values from -0.25 to 0.25
- weight_memory: float32 [3, 512, 1024], P(None, ('seq', 'grp')), may hold values from -0.15625 to 0.15625
- weight_out: float32 [512, 512], P(('seq', 'grp')), may hold values from -1.5 to 1.5
- weight_up: float32 [512, 2048], P(('seq', 'grp')), may hold values from -0.25 to 0.25
- weight_down: float32 [2048, 512], P(('seq', 'grp')), may hold values from -0.125 to 0.125
- vectors: float32 [9, 512], P(None, ('seq', 'grp')), may hold values from -0.5 to 1.5, as said below
- first_query: float32 [512, 512], P(('seq', 'grp')), may hold values from -64 to 64
- first_memory: float32 [3, 512, 1024], P(None, ('seq', 'grp')), may hold values from -40 to 40
- first_out: float32 [512, 512], P(('seq', 'grp')), may hold values from -24 to 24
- first_up: float32 [512, 2048], P(('seq', 'grp')), may hold values from -40 to 40
- first_down: float32 [2048, 512], P(('seq', 'grp')), may hold values from -80 to 80
- first_vectors: float32 [9, 512], P(None, ('seq', 'grp')), may hold values from -128 to 128
- second_query: float32 [512, 512], P(('seq', 'grp')), may hold values from 484.7616 to 1939.0464
- second_memory: float32 [3, 512, 1024], P(None, ('seq', 'grp')), may hold values from 174.36671 to 696.7296
- second_out: float32 [512, 512], P(('seq', 'grp')), may hold values from 77.4144 to 309.6576
- second_up: float32 [512, 2048], P(('seq', 'grp')), may hold values from 174.36671 to 696.7296
- second_down: float32 [2048, 512], P(('seq', 'grp')), may hold values from 696.7296 to 2790.6047
- second_vectors: float32 [9, 512], P(None, ('seq', 'grp')), may hold values from 1939.0464 to 7741.44
Outputs:
- out_tokens: bfloat16 [8, 4608, 512], P('grp', 'seq')
- grad_tokens: bfloat16 [8, 4608, 512], P('grp', 'seq')
- moment_query: float32 [512, 512], P(('seq', 'grp'))
- moment_memory: float32 [3, 512, 1024], P(None, ('seq', 'grp'))
- moment_out: float32 [512, 512], P(('seq', 'grp'))
- moment_up: float32 [512, 2048], P(('seq', 'grp'))
- moment_down: float32 [2048, 512], P(('seq', 'grp'))
- moment_vectors: float32 [9, 512], P(None, ('seq', 'grp'))
- square_query: float32 [512, 512], P(('seq', 'grp'))
- square_memory: float32 [3, 512, 1024], P(None, ('seq', 'grp'))
- square_out: float32 [512, 512], P(('seq', 'grp'))
- square_up: float32 [512, 2048], P(('seq', 'grp'))
- square_down: float32 [2048, 512], P(('seq', 'grp'))
- square_vectors: float32 [9, 512], P(None, ('seq', 'grp'))
- master_query: float32 [512, 512], P(('seq', 'grp'))
- master_memory: float32 [3, 512, 1024], P(None, ('seq', 'grp'))
- master_out: float32 [512, 512], P(('seq', 'grp'))
- master_up: float32 [512, 2048], P(('seq', 'grp'))
- master_down: float32 [2048, 512], P(('seq', 'grp'))
- master_vectors: float32 [9, 512], P(None, ('seq', 'grp'))
- copy_query: bfloat16 [512, 512], P(('seq', 'grp'))
- copy_memory: bfloat16 [3, 512, 1024], P(None, ('seq', 'grp'))
- copy_out: bfloat16 [512, 512], P(('seq', 'grp'))
- copy_up: bfloat16 [512, 2048], P(('seq', 'grp'))
- copy_down: bfloat16 [2048, 512], P(('seq', 'grp'))
- copy_vectors: bfloat16 [9, 512], P(None, ('seq', 'grp'))
Inputs may be any that keep to these rules, and one draw needn't show every extreme that they name: `lengths`: every sequence has more than 3456 live positions; some sequence fills all 4608. `vectors`: rows 0 and 2 lie between 0.5 and 1.5, the other rows between -0.5 and 0.5.
All inputs are finite; a program needn't handle non-finite values.
Results may differ from a plain program's by a relative error of at most 0.012.
The roundings to bfloat16 on the way count: a program that leaves them out, or rounds other values in their place, can miss the bound.
Values may be sent and summed in bfloat16 or wider, within the bound.
A program may use at most 128 MiB of HBM per device.

v0:
```python
import jax
import jax.numpy as jnp
from jax import lax
from jax.sharding import PartitionSpec as P

H = 8
STEP = 10


NORM_EPSILON = 1e-05
BETA_FIRST = 0.9
BETA_SECOND = 0.95
ADAM_EPSILON = 1e-08
WEIGHT_DECAY = 0.1
LEARNING_RATES = (0.05, 0.04, 0.3, 0.05, 0.03, 0.5)
MASKED_SCORE = -1e30


def from_behind(x, axis, by):
    peers = lax.axis_size(axis)
    pairs = [(i, i + by) for i in range(peers) if 0 <= i + by < peers]
    return lax.ppermute(x, axis, pairs)


def matmul(left, right):
    return jnp.dot(left, right, preferred_element_type=jnp.float32)


def over_rows(left, right):
    return lax.dot_general(
        left, right, (((0,), (0,)), ((), ())), preferred_element_type=jnp.float32
    )


def against(left, right):
    return lax.dot_general(
        left, right, (((1,), (1,)), ((), ())), preferred_element_type=jnp.float32
    )


def norm_forward(values, gain, shift):
    centred = values - jnp.mean(values, axis=-1, keepdims=True)
    factor = lax.rsqrt(jnp.mean(centred * centred, axis=-1, keepdims=True) + NORM_EPSILON)
    unit_rows = centred * factor
    return (unit_rows * gain + shift, unit_rows, factor)


def norm_backward(upstream, unit_rows, factor, gain):
    scaled = upstream * gain
    inward = factor * (
        scaled
        - jnp.mean(scaled, axis=-1, keepdims=True)
        - unit_rows * jnp.mean(scaled * unit_rows, axis=-1, keepdims=True)
    )
    return (inward, jnp.sum(upstream * unit_rows, axis=0), jnp.sum(upstream, axis=0))


def masked_scores(query_tile_rows, key_row_block, positions):
    slot_starts = 3 * jnp.arange(key_row_block.shape[0], dtype=jnp.int32)
    score_matrix = jnp.einsum(
        "azv,lzv->zal", query_tile_rows, key_row_block, preferred_element_type=jnp.float32
    ) * query_tile_rows.shape[2] ** (-0.5)
    visible = slot_starts[None, :] <= positions[:, None]
    return jnp.where(visible[None], score_matrix, MASKED_SCORE)


def attend_forward(queries, key_row_block, value_row_block, anchor, block_rows):
    block_count = queries.shape[0] // block_rows
    offsets = block_rows * jnp.arange(block_count, dtype=jnp.int32)

    def attend_block(inputs):
        query_tile_rows, offset_rows = inputs
        score_matrix = masked_scores(
            query_tile_rows,
            key_row_block,
            anchor + offset_rows + jnp.arange(block_rows, dtype=jnp.int32),
        )
        highest = jnp.max(score_matrix, axis=-1, keepdims=True)
        exponent = jnp.exp(score_matrix - highest)
        summed = jnp.sum(exponent, axis=-1, keepdims=True)
        reduced_weights = (exponent / summed).astype(jnp.bfloat16)
        mixed = jnp.einsum(
            "yup,pyb->uyb", reduced_weights, value_row_block, preferred_element_type=jnp.float32
        )
        return (mixed, (highest + jnp.log(summed))[..., 0])

    blocks_in = queries.reshape(block_count, block_rows, queries.shape[1], queries.shape[2])
    mixed, logsum = lax.map(attend_block, (blocks_in, offsets))
    return (mixed.reshape(queries.shape), logsum)


def attend_backward(queries, key_row_block, value_row_block, upstream, logsum, anchor, block_rows):
    block_count = queries.shape[0] // block_rows
    offsets = block_rows * jnp.arange(block_count, dtype=jnp.int32)
    scale_factor = queries.shape[2] ** (-0.5)

    def attend_back(carry, inputs):
        grad_keys, grad_values = carry
        query_tile_rows, incoming_gradient_rows, logsum_block, offset_rows = inputs
        score_matrix = masked_scores(
            query_tile_rows,
            key_row_block,
            anchor + offset_rows + jnp.arange(block_rows, dtype=jnp.int32),
        )
        weights_soft = jnp.exp(score_matrix - logsum_block[..., None])
        grad_weights = jnp.einsum(
            "azv,lzv->zal",
            incoming_gradient_rows,
            value_row_block,
            preferred_element_type=jnp.float32,
        )
        centre = jnp.sum(weights_soft * grad_weights, axis=-1, keepdims=True)
        score_gradient = (weights_soft * (grad_weights - centre)).astype(jnp.bfloat16)
        grad_query = (
            jnp.einsum(
                "yup,pyb->uyb", score_gradient, key_row_block, preferred_element_type=jnp.float32
            )
            * scale_factor
        )
        grad_keys = (
            grad_keys
            + jnp.einsum(
                "xof,oxa->fxa", score_gradient, query_tile_rows, preferred_element_type=jnp.float32
            )
            * scale_factor
        )
        grad_values = grad_values + jnp.einsum(
            "xof,oxa->fxa",
            weights_soft.astype(jnp.bfloat16),
            incoming_gradient_rows,
            preferred_element_type=jnp.float32,
        )
        return ((grad_keys, grad_values), grad_query)

    shape_blocks = (block_count, block_rows, queries.shape[1], queries.shape[2])
    zeros_init = jnp.zeros(key_row_block.shape, jnp.float32)
    (grad_keys, grad_values), grad_query = lax.scan(
        attend_back,
        (zeros_init, zeros_init),
        (queries.reshape(shape_blocks), upstream.reshape(shape_blocks), logsum, offsets),
    )
    return (grad_query.reshape(queries.shape), grad_keys, grad_values)


def adamw(weight, gradient, moment, square, step_rate):
    moment_new = BETA_FIRST * moment + (1.0 - BETA_FIRST) * gradient
    square_new = BETA_SECOND * square + (1.0 - BETA_SECOND) * gradient * gradient
    fixed_first = 1.0 - BETA_FIRST**STEP
    fixed_second = 1.0 - BETA_SECOND**STEP
    update = (
        moment_new / fixed_first / (jnp.sqrt(square_new / fixed_second) + ADAM_EPSILON)
        + WEIGHT_DECAY * weight
    )
    master = weight - step_rate * update
    return (moment_new, square_new, master, master.astype(jnp.bfloat16))


def body(
    tokens,
    cotangent,
    lengths,
    weight_query,
    weight_memory,
    weight_out,
    weight_up,
    weight_down,
    vectors,
    first_query,
    first_memory,
    first_out,
    first_up,
    first_down,
    first_vectors,
    second_query,
    second_memory,
    second_out,
    second_up,
    second_down,
    second_vectors,
):
    gathered = (
        lax.all_gather(weight_query.astype(jnp.bfloat16), ("seq", "grp"), axis=0, tiled=True),
        lax.all_gather(weight_memory.astype(jnp.bfloat16), ("seq", "grp"), axis=1, tiled=True),
        lax.all_gather(weight_out.astype(jnp.bfloat16), ("seq", "grp"), axis=0, tiled=True),
        lax.all_gather(weight_up.astype(jnp.bfloat16), ("seq", "grp"), axis=0, tiled=True),
        lax.all_gather(weight_down.astype(jnp.bfloat16), ("seq", "grp"), axis=0, tiled=True),
        lax.all_gather(vectors.astype(jnp.bfloat16), ("seq", "grp"), axis=1, tiled=True),
    )
    query_w, memory_w, out_w, up_w, down_w, vector_low = gathered
    vector_rows = vector_low.astype(jnp.float32)
    model_width = query_w.shape[0]
    hidden_units = up_w.shape[1]
    head_size = model_width // H
    seq_count = lax.axis_size("seq")
    seq_index = lax.axis_index("seq")
    local_rows = tokens.shape[1]
    local_slots = local_rows // 3
    inputs = tokens[0].astype(jnp.float32)
    normed, unit_one, factor_one = norm_forward(inputs, vector_rows[0], vector_rows[1])
    normed_low = normed.astype(jnp.bfloat16)
    queries = matmul(normed_low, query_w).astype(jnp.bfloat16)
    borrowed = from_behind(normed_low[local_rows - 2 :], "seq", 1)
    extended = jnp.concatenate([borrowed, normed_low], axis=0)
    windows = extended[:local_rows].reshape(local_slots, 3 * model_width)
    memory_flat = memory_w.reshape(3 * model_width, 2 * model_width)
    memory = matmul(windows, memory_flat).astype(jnp.bfloat16)
    share_width = model_width // seq_count
    local_heads = H // seq_count
    head_queries, head_memory = (
        lax.all_to_all(
            queries.reshape(local_rows, 1, seq_count, share_width),
            "seq",
            split_axis=2,
            concat_axis=0,
            tiled=True,
        ),
        lax.all_to_all(
            memory.reshape(local_slots, 2, seq_count, share_width),
            "seq",
            split_axis=2,
            concat_axis=0,
            tiled=True,
        ),
    )
    total_rows = head_queries.shape[0]
    total_slots = head_memory.shape[0]
    query_heads = head_queries.reshape(total_rows, local_heads, head_size)
    key_heads = head_memory[:, 0].reshape(total_slots, local_heads, head_size)
    value_heads = head_memory[:, 1].reshape(total_slots, local_heads, head_size)
    block_rows = min(512, total_rows)
    mixed, logsum = attend_forward(query_heads, key_heads, value_heads, 0, block_rows)
    mixed_low = mixed.astype(jnp.bfloat16).reshape(total_rows, 1, share_width)
    attended = lax.all_to_all(mixed_low, "seq", split_axis=0, concat_axis=1, tiled=True).reshape(
        local_rows, model_width
    )
    residual = inputs + matmul(attended, out_w)
    normed_two, unit_two, factor_two = norm_forward(residual, vector_rows[2], vector_rows[3])
    normed_two_low = normed_two.astype(jnp.bfloat16)
    pre_act = matmul(normed_two_low, up_w) + vector_rows[5:].reshape(hidden_units)
    activated, gelu_pull = jax.vjp(jax.nn.gelu, pre_act)
    activated_low = activated.astype(jnp.bfloat16)
    result = residual + matmul(activated_low, down_w) + vector_rows[4]
    positions = seq_index * local_rows + jnp.arange(local_rows, dtype=jnp.int32)
    live_mask = (positions < lengths[0]).astype(jnp.float32)
    grad_out = cotangent[0].astype(jnp.float32) * live_mask[:, None]
    grad_out_low = grad_out.astype(jnp.bfloat16)
    grad_down = over_rows(activated_low, grad_out_low)
    grad_activated = against(grad_out_low, down_w)
    grad_pre_low = gelu_pull(grad_activated)[0].astype(jnp.bfloat16)
    grad_up = over_rows(normed_two_low, grad_pre_low)
    grad_up_bias = jnp.sum(grad_pre_low.astype(jnp.float32), axis=0)
    grad_normed_two = against(grad_pre_low, up_w)
    grad_norm_two, grad_gain_two, grad_shift_two = norm_backward(
        grad_normed_two, unit_two, factor_two, vector_rows[2]
    )
    grad_residual = grad_out + grad_norm_two
    grad_branch_low = grad_residual.astype(jnp.bfloat16)
    grad_outw = over_rows(attended, grad_branch_low)
    grad_attended_low = against(grad_branch_low, out_w).astype(jnp.bfloat16)
    grad_heads = lax.all_to_all(
        grad_attended_low.reshape(local_rows, 1, seq_count, share_width),
        "seq",
        split_axis=2,
        concat_axis=0,
        tiled=True,
    ).reshape(total_rows, local_heads, head_size)
    grad_q, grad_k, grad_v = attend_backward(
        query_heads, key_heads, value_heads, grad_heads, logsum, 0, block_rows
    )
    packed = (
        jnp.stack([grad_k, grad_v], axis=1)
        .astype(jnp.bfloat16)
        .reshape(total_slots, 2, 1, share_width)
    )
    token_queries, token_memory = (
        lax.all_to_all(
            grad_q.astype(jnp.bfloat16).reshape(total_rows, 1, 1, share_width),
            "seq",
            split_axis=0,
            concat_axis=2,
            tiled=True,
        ),
        lax.all_to_all(packed, "seq", split_axis=0, concat_axis=2, tiled=True),
    )
    grad_queries_low = token_queries.reshape(local_rows, model_width)
    grad_memory_low = token_memory.reshape(local_slots, 2 * model_width)
    grad_queryw = over_rows(normed_low, grad_queries_low)
    grad_normed = against(grad_queries_low, query_w)
    grad_memoryw = over_rows(windows, grad_memory_low).reshape(3, model_width, 2 * model_width)
    grad_windows = against(grad_memory_low, memory_flat).reshape(local_rows, model_width)
    returned = from_behind(grad_windows[:2], "seq", -1)
    grad_normed = grad_normed + jnp.concatenate([grad_windows[2:], returned], axis=0)
    grad_norm_one, grad_gain_one, grad_shift_one = norm_backward(
        grad_normed, unit_one, factor_one, vector_rows[0]
    )
    grad_inputs = (grad_residual + grad_norm_one).astype(jnp.bfloat16)
    grad_vector_rows = jnp.concatenate(
        [
            jnp.stack(
                [
                    grad_gain_one,
                    grad_shift_one,
                    grad_gain_two,
                    grad_shift_two,
                    jnp.sum(grad_out, axis=0),
                ]
            ),
            grad_up_bias.reshape(4, model_width),
        ],
        axis=0,
    )
    reduced = (
        lax.psum_scatter(grad_queryw, ("seq", "grp"), scatter_dimension=0, tiled=True),
        lax.psum_scatter(grad_memoryw, ("seq", "grp"), scatter_dimension=1, tiled=True),
        lax.psum_scatter(grad_outw, ("seq", "grp"), scatter_dimension=0, tiled=True),
        lax.psum_scatter(grad_up, ("seq", "grp"), scatter_dimension=0, tiled=True),
        lax.psum_scatter(grad_down, ("seq", "grp"), scatter_dimension=0, tiled=True),
        lax.psum_scatter(grad_vector_rows, ("seq", "grp"), scatter_dimension=1, tiled=True),
    )
    new_query = adamw(weight_query, reduced[0], first_query, second_query, LEARNING_RATES[0])
    new_memory = adamw(weight_memory, reduced[1], first_memory, second_memory, LEARNING_RATES[1])
    new_out = adamw(weight_out, reduced[2], first_out, second_out, LEARNING_RATES[2])
    new_up = adamw(weight_up, reduced[3], first_up, second_up, LEARNING_RATES[3])
    new_down = adamw(weight_down, reduced[4], first_down, second_down, LEARNING_RATES[4])
    new_vectors = adamw(vectors, reduced[5], first_vectors, second_vectors, LEARNING_RATES[5])
    return (
        result.astype(jnp.bfloat16)[None],
        grad_inputs[None],
        new_query[0],
        new_memory[0],
        new_out[0],
        new_up[0],
        new_down[0],
        new_vectors[0],
        new_query[1],
        new_memory[1],
        new_out[1],
        new_up[1],
        new_down[1],
        new_vectors[1],
        new_query[2],
        new_memory[2],
        new_out[2],
        new_up[2],
        new_down[2],
        new_vectors[2],
        new_query[3],
        new_memory[3],
        new_out[3],
        new_up[3],
        new_down[3],
        new_vectors[3],
    )


def solution(mesh):
    in_specs = (
        P("grp", "seq", None),
        P("grp", "seq", None),
        P("grp"),
        P(("seq", "grp"), None),
        P(None, ("seq", "grp"), None),
        P(("seq", "grp"), None),
        P(("seq", "grp"), None),
        P(("seq", "grp"), None),
        P(None, ("seq", "grp")),
        P(("seq", "grp"), None),
        P(None, ("seq", "grp"), None),
        P(("seq", "grp"), None),
        P(("seq", "grp"), None),
        P(("seq", "grp"), None),
        P(None, ("seq", "grp")),
        P(("seq", "grp"), None),
        P(None, ("seq", "grp"), None),
        P(("seq", "grp"), None),
        P(("seq", "grp"), None),
        P(("seq", "grp"), None),
        P(None, ("seq", "grp")),
    )
    out_specs = (
        P("grp", "seq", None),
        P("grp", "seq", None),
        P(("seq", "grp"), None),
        P(None, ("seq", "grp"), None),
        P(("seq", "grp"), None),
        P(("seq", "grp"), None),
        P(("seq", "grp"), None),
        P(None, ("seq", "grp")),
        P(("seq", "grp"), None),
        P(None, ("seq", "grp"), None),
        P(("seq", "grp"), None),
        P(("seq", "grp"), None),
        P(("seq", "grp"), None),
        P(None, ("seq", "grp")),
        P(("seq", "grp"), None),
        P(None, ("seq", "grp"), None),
        P(("seq", "grp"), None),
        P(("seq", "grp"), None),
        P(("seq", "grp"), None),
        P(None, ("seq", "grp")),
        P(("seq", "grp"), None),
        P(None, ("seq", "grp"), None),
        P(("seq", "grp"), None),
        P(("seq", "grp"), None),
        P(("seq", "grp"), None),
        P(None, ("seq", "grp")),
    )
    return jax.shard_map(body, mesh=mesh, in_specs=in_specs, out_specs=out_specs, check_vma=False)
```

profile of v0, /device:TPU:0, one launch (start us, length us, event | category | flops | bytes accessed | tf_op | source)
XLA Modules:
  0.0 1525.4 jit_solution(631971996852980865)
XLA Ops:
  10.4 43.9 %all_gather.18 = bf16[9,512]{0,1:T(8,128)(2,1)S(1)} all-gather(bf16[9,16]{0,1:T(8,128)(2,1)S(1)} %copy.182), channel_id=1, replica_groups=mesh['seq'=4,'grp'=8] {'seq','grp'}, dimensions={1}, use_global_device_ids=true | all-gather | bytes 9504 | tf_op jit(solution)/shard_map/all_gather | solution.py:187
  58.5 39.5 %all_gather.19 = bf16[512,512]{1,0:T(8,128)(2,1)S(1)} all-gather(bf16[16,512]{1,0:T(8,128)(2,1)S(1)} %convert_element_type.148), channel_id=1, replica_groups=mesh['seq'=4,'grp'=8] {'seq','grp'}, dimensions={0}, use_global_device_ids=true | all-gather | bytes 540672 | tf_op jit(solution)/shard_map/all_gather | solution.py:182
  108.7 12.4 collective-permute-done
  127.4 4.6 convolution_convert_fusion.2
  135.0 4.9 all-to-all-start.1
  153.5 85.8 %while.27 = (s32[]{:T(128)}, bf16[9,512,2,64]{1,3,2,0:T(8,128)(2,1)}, f32[9,2,512]{2,1,0:T(2,128)}, s32[9]{0:T(128)S(1)}, bf16[9,512,2,64]{1,3,2,0:T(8,128)(2,1)...) while((s32[]{:T(128)}, bf16[9,512,2,64]{1,3,2,0:T(8,128)(2,1)}, ...), condition=%wide.region_5.6_spmd, body=%wide.region_2.5_spmd.sunk | while | flops 422315008 | bytes 23249016 | solution.py:88
  239.4 6.4 copy.217
  245.8 9.7 reshape.334
  256.0 26.2 %reduce.11 = bf16[4608,128]{1,0:T(8,128)(2,1)S(1)} reduce(bf16[4608,1,128]{2,1,0:T(2,128)(2,1)} %reshape.334, bf16[]{:T(256)} %broadcast.365), dimensions={1}, to_apply=%reshape.334.reduce_sub_computation | reduce | bytes 2359298 | tf_op jit(solution)/shard_map/convert_element_type | solution.py:232
  290.8 41.4 %all_gather.21 = bf16[512,512]{1,0:T(8,128)(2,1)S(1)} all-gather(bf16[16,512]{1,0:T(8,128)(2,1)S(1)} %convert_element_type.154), channel_id=1, replica_groups=mesh['seq'=4,'grp'=8] {'seq','grp'}, dimensions={0}, use_global_device_ids=true | all-gather | bytes 540672 | tf_op jit(solution)/shard_map/all_gather | solution.py:184
  342.0 5.3 convolution_add_fusion
  350.9 5.8 fusion.77
  357.3 139.1 %reduce-scatter.17.cloned.1.call-done = f32[64,512]{1,0:T(8,128)} async-done(((f32[2048,512]{1,0:T(8,128)}), f32[64,512]{1,0:T(8,128)}) %reduce-scatter.17.cloned.1.call-update) | async-done | bytes 131088 | tf_op jit(solution)/shard_map/reduce_scatter | solution.py:317
  498.2 54.9 %all-gather.8.cloned.1.call-done = bf16[2048,512]{1,0:T(8,128)(2,1)} async-done(((bf16[64,512]{1,0:T(8,128)(2,1)}), bf16[2048,512]{1,0:T(8,128)(2,1)}) %all-gather.8.cloned.1.call-update) | async-done | bytes 2097168 | tf_op jit(solution)/shard_map/all_gather | solution.py:186
  553.1 11.7 convert_reduce_fusion
  564.8 4.7 fusion.105
  584.6 15.7 %all-to-all-done.3 = bf16[1152,1,4,128]{0,3,1,2:T(8,128)(2,1)S(1)} async-done(((bf16[1152,1,4,128]{0,3,1,2:T(8,128)(2,1)}), bf16[1152,1,4,128]{0,3,1,2:T(8,128)(2,1)S(1)}, u32[]{:S(2)}, u32[]{:S(2)}) %all-to-all-start.3) | async-done | bytes 1179680 | tf_op jit(solution)/shard_map/all_to_all | solution.py:260
  607.9 131.7 %while.28 = (s32[]{:T(128)}, f32[1536,2,64]{0,2,1:T(8,128)}, f32[1536,2,64]{0,2,1:T(8,128)}, bf16[9,512,2,64]{1,3,2,0:T(8,128)(2,1)}, bf16[9,512,2,64]{1,3,2,0:T...) while((s32[]{:T(128)}, f32[1536,2,64]{0,2,1:T(8,128)}, ...), condition=%wide.region_12.13_spmd.clone, body=%wide.region_10.12_spmd.clone.sunk | while | flops 1022624768 | bytes 66490652 | solution.py:137
  743.8 4.4 all-to-all-start.5
  748.2 4.5 copy.218
  752.7 8.6 reshape.335
  761.2 25.1 %reduce.12 = bf16[4608,128]{1,0:T(8,128)(2,1)S(1)} reduce(bf16[4608,1,1,128]{3,2,1,0:T(2,128)(2,1)S(1)} %reshape.335, bf16[]{:T(256)} %broadcast.365), dimensions={1,2}, to_apply=%reshape.335.reduce_sub_computation | reduce | bytes 2359298 | tf_op jit(solution)/shard_map/convert_element_type | solution.py:277
  795.2 4.7 fusion.106
  816.2 5.7 fusion.60
  833.3 7.0 fusion.90
  845.2 5.9 fusion.107
  851.8 9.3 fusion.52
  871.2 91.3 %reduce-scatter.19.cloned.1.call-done = f32[16,9]{1,0:T(8,128)} async-done(((f32[512,9]{1,0:T(8,128)}), f32[16,9]{1,0:T(8,128)}) %reduce-scatter.19.cloned.1.call-update) | async-done | bytes 592
  963.9 131.9 %reduce-scatter.13.cloned.1.call-done = f32[16,512]{1,0:T(8,128)} async-done(((f32[512,512]{1,0:T(8,128)}), f32[16,512]{1,0:T(8,128)}) %reduce-scatter.13.cloned.1.call-update) | async-done | bytes 32784 | tf_op jit(solution)/shard_map/reduce_scatter | solution.py:315
  1097.2 132.0 %reduce-scatter.9.cloned.1.call-done = f32[16,512]{1,0:T(8,128)} async-done(((f32[512,512]{1,0:T(8,128)}), f32[16,512]{1,0:T(8,128)}) %reduce-scatter.9.cloned.1.call-update) | async-done | bytes 32784 | tf_op jit(solution)/shard_map/reduce_scatter | solution.py:313
  1230.6 139.3 %reduce-scatter.15.cloned.1.call-done = f32[16,2048]{1,0:T(8,128)} async-done(((f32[512,2048]{1,0:T(8,128)}), f32[16,2048]{1,0:T(8,128)}) %reduce-scatter.15.cloned.1.call-update) | async-done | bytes 131088 | tf_op jit(solution)/shard_map/reduce_scatter | solution.py:316
  1371.7 144.9 %reduce-scatter.11.cloned.1.call-done = f32[3,16,1024]{2,1,0:T(8,128)} async-done(((f32[3,512,1024]{2,1,0:T(8,128)}), f32[3,16,1024]{2,1,0:T(8,128)}) %reduce-scatter.11.cloned.1.call-update) | async-done | bytes 196624 | tf_op jit(solution)/shard_map/reduce_scatter | solution.py:314
  (475 shorter events, 367.7 us)
Async XLA Ops:
  7.2 120.2 %all-gather.4.cloned.1.call-start = ((), (), s32[]{:S(2)}) async-start(), calls=%async_computation.12 | async-start | bytes 3244032 | tf_op jit(solution)/shard_map/all_gather | solution.py:183
  56.7 282.5 %copy-start = (bf16[1,1152,512]{1,2,0:T(8,128)(2,1)}, bf16[1,1152,512]{1,2,0:T(8,128)(2,1)S(1)}, u32[]{:S(2)}) copy-start(bf16[1,1152,512]{1,2,0:T(8,128)(2,1)S(1)} %copy.181) | copy-start | bytes 3538948
  57.9 284.0 %copy-start.53 = (f32[512]{0:T(512)}, f32[512]{0:T(512)S(1)}, u32[]{:S(2)}) copy-start(f32[512]{0:T(512)S(1)} %get-tuple-element.406) | copy-start | bytes 6148
  57.9 518.0 %copy-start.46 = (f32[512]{0:T(512)}, f32[512]{0:T(512)S(1)}, u32[]{:S(2)}) copy-start(f32[512]{0:T(512)S(1)} %get-tuple-element.404) | copy-start | bytes 6148
  100.4 34.5 %all-to-all-start = ((bf16[1152,1,4,128]{0,3,1,2:T(8,128)(2,1)}), bf16[1152,1,4,128]{0,3,1,2:T(8,128)(2,1)}, u32[]{:S(2)}, u32[]{:S(2)}) async-start(bf16[1152,1,4,128]{0,3,1,2:T(8,128)(2,1)} %bitcast.233), calls=%async_computation | async-start | bytes 2359296 | tf_op jit(solution)/shard_map/all_to_all | solution.py:210
  104.8 16.3 %collective-permute-start = (bf16[2,512]{0,1:T(8,128)(2,1)S(1)}, bf16[2,512]{0,1:T(8,128)(2,1)S(1)}, u32[]{:S(2)}, u32[]{:S(2)}) collective-permute-start(bf16[2,512]{0,1:T(8,128)(2,1)S(1)} %slice.52), channel_id=1, source_target_pairs={{0,8},{8,16},{16,24},{1,9},{9,17},{17,25},{2,10},{10,18},{18,26},{... | collective-permute-start | bytes 6152 | tf_op jit(solution)/shard_map/ppermute | solution.py:22
  135.0 16.1 %all-to-all-start.1 = ((bf16[384,2,4,128]{3,0,1,2:T(8,128)(2,1)}), bf16[384,2,4,128]{3,0,1,2:T(8,128)(2,1)S(1)}, u32[]{:S(2)}, u32[]{:S(2)}) async-start(bf16[384,2,4,128]{3,0,1,2:T(8,128)(2,1)} %copy.186), calls=%async_computation.1 | async-start | bytes 1572864 | tf_op jit(solution)/shard_map/all_to_all | solution.py:217
  139.9 202.1 %all-gather.6.cloned.1.call-start = ((), (), s32[]{:S(2)}) async-start(), calls=%async_computation.13 | async-start | bytes 2162688 | tf_op jit(solution)/shard_map/all_gather | solution.py:185
  283.9 48.3 %all-to-all-start.2 = ((bf16[4,2,73728]{2,1,0:T(2,128)(2,1)}), bf16[4,2,73728]{2,1,0:T(2,128)(2,1)S(1)}, u32[]{:S(2)}, u32[]{:S(2)}) async-start(bf16[4,2,73728]{2,1,0:T(2,128)(2,1)} %reshape.344), calls=%async_computation.2 | async-start | bytes 2359296 | tf_op jit(solution)/shard_map/all_to_all | solution.py:233
  287.4 209.0 %reduce-scatter.17.cloned.1.call-start = ((), (), s32[]{:S(2)}) async-start(), calls=%async_computation.19 | async-start | bytes 4325376 | tf_op jit(solution)/shard_map/reduce_scatter | solution.py:317
  341.9 234.0 %copy-start.40 = (f32[1152]{0:T(1024)}, f32[1152]{0:T(1024)S(1)}, u32[]{:S(2)}) copy-start(f32[1152]{0:T(1024)S(1)} %add_rsqrt_fusion) | copy-start | bytes 13828
  356.8 196.3 %all-gather.8.cloned.1.call-start = ((), (), s32[]{:S(2)}) async-start(), calls=%async_computation.14 | async-start | bytes 2162688 | tf_op jit(solution)/shard_map/all_gather | solution.py:186
  580.9 19.4 %all-to-all-start.3 = ((bf16[1152,1,4,128]{0,3,1,2:T(8,128)(2,1)}), bf16[1152,1,4,128]{0,3,1,2:T(8,128)(2,1)S(1)}, u32[]{:S(2)}, u32[]{:S(2)}) async-start(bf16[1152,1,4,128]{0,3,1,2:T(8,128)(2,1)} %bitcast.24), calls=%async_computation.3 | async-start | bytes 2359296 | tf_op jit(solution)/shard_map/all_to_all | solution.py:260
  743.8 44.3 %all-to-all-start.5 = ((bf16[1536,2,1,128]{3,1,2,0:T(2,128)(2,1)}), bf16[1536,2,1,128]{3,1,2,0:T(2,128)(2,1)}, u32[]{:S(2)}, u32[]{:S(2)}) async-start(bf16[1536,2,1,128]{3,1,2,0:T(2,128)(2,1)} %copy.205), calls=%async_computation.5 | async-start | bytes 1572864 | tf_op jit(solution)/shard_map/all_to_all | solution.py:283
  788.1 21.8 %all-to-all-start.4 = ((bf16[4,2,73728]{2,1,0:T(2,128)(2,1)}), bf16[4,2,73728]{2,1,0:T(2,128)(2,1)}, u32[]{:S(2)}, u32[]{:S(2)}) async-start(bf16[4,2,73728]{2,1,0:T(2,128)(2,1)} %reshape.346), calls=%async_computation.4 | async-start | bytes 2359296 | tf_op jit(solution)/shard_map/all_to_all | solution.py:276
  792.4 170.1 %reduce-scatter.19.cloned.1.call-start = ((), (), s32[]{:S(2)}) async-start(), calls=%async_computation.20 | async-start | bytes 270336
  803.2 13.0 collective-permute-start.1
  826.3 269.5 %reduce-scatter.13.cloned.1.call-start = ((), (), s32[]{:S(2)}) async-start(), calls=%async_computation.17 | async-start | bytes 1081344 | tf_op jit(solution)/shard_map/reduce_scatter | solution.py:315
  829.8 399.4 %reduce-scatter.9.cloned.1.call-start = ((), (), s32[]{:S(2)}) async-start(), calls=%async_computation.15 | async-start | bytes 1081344 | tf_op jit(solution)/shard_map/reduce_scatter | solution.py:313
  833.3 536.7 %reduce-scatter.15.cloned.1.call-start = ((), (), s32[]{:S(2)}) async-start(), calls=%async_computation.18 | async-start | bytes 4325376 | tf_op jit(solution)/shard_map/reduce_scatter | solution.py:316
  840.4 676.2 %reduce-scatter.11.cloned.1.call-start = ((), (), s32[]{:S(2)}) async-start(), calls=%async_computation.16 | async-start | bytes 6488064 | tf_op jit(solution)/shard_map/reduce_scatter | solution.py:314
  868.5 227.3 %copy-start.31 = (f32[16,512]{1,0:T(8,128)S(1)}, f32[16,512]{1,0:T(8,128)}, u32[]{:S(2)}) copy-start(f32[16,512]{1,0:T(8,128)} %param.30) | copy-start | bytes 98308
  868.5 227.3 %copy-start.41 = (f32[16,512]{1,0:T(8,128)S(1)}, f32[16,512]{1,0:T(8,128)}, u32[]{:S(2)}) copy-start(f32[16,512]{1,0:T(8,128)} %param.42) | copy-start | bytes 98308
  868.6 360.7 %copy-start.32 = (f32[16,512]{1,0:T(8,128)S(1)}, f32[16,512]{1,0:T(8,128)}, u32[]{:S(2)}) copy-start(f32[16,512]{1,0:T(8,128)} %param.28) | copy-start | bytes 98308
  868.6 360.7 %copy-start.43 = (f32[16,512]{1,0:T(8,128)S(1)}, f32[16,512]{1,0:T(8,128)}, u32[]{:S(2)}) copy-start(f32[16,512]{1,0:T(8,128)} %param.40) | copy-start | bytes 98308
  868.6 360.6 %copy-start.44 = (f32[16,512]{1,0:T(8,128)S(1)}, f32[16,512]{1,0:T(8,128)}, u32[]{:S(2)}) copy-start(f32[16,512]{1,0:T(8,128)} %param.34) | copy-start | bytes 98308
  868.6 501.4 %copy-start.24 = (f32[16,2048]{1,0:T(8,128)S(1)}, f32[16,2048]{1,0:T(8,128)}, u32[]{:S(2)}) copy-start(f32[16,2048]{1,0:T(8,128)} %param.31) | copy-start | bytes 393220
  868.6 501.4 %copy-start.28 = (f32[16,2048]{1,0:T(8,128)S(1)}, f32[16,2048]{1,0:T(8,128)}, u32[]{:S(2)}) copy-start(f32[16,2048]{1,0:T(8,128)} %param.43) | copy-start | bytes 393220
  868.6 501.4 %copy-start.29 = (f32[16,2048]{1,0:T(8,128)S(1)}, f32[16,2048]{1,0:T(8,128)}, u32[]{:S(2)}) copy-start(f32[16,2048]{1,0:T(8,128)} %param.37) | copy-start | bytes 393220
  868.6 648.0 %copy-start.22 = (f32[3,16,1024]{2,1,0:T(8,128)S(1)}, f32[3,16,1024]{2,1,0:T(8,128)}, u32[]{:S(2)}) copy-start(f32[3,16,1024]{2,1,0:T(8,128)} %param.29) | copy-start | bytes 589828
  868.6 648.0 %copy-start.26 = (f32[3,16,1024]{2,1,0:T(8,128)S(1)}, f32[3,16,1024]{2,1,0:T(8,128)}, u32[]{:S(2)}) copy-start(f32[3,16,1024]{2,1,0:T(8,128)} %param.41) | copy-start | bytes 589828
  868.7 647.9 %copy-start.27 = (f32[3,16,1024]{2,1,0:T(8,128)S(1)}, f32[3,16,1024]{2,1,0:T(8,128)}, u32[]{:S(2)}) copy-start(f32[3,16,1024]{2,1,0:T(8,128)} %param.35) | copy-start | bytes 589828
  (76 other events, 1299.7 us)
Sparse Core Ops, SparseCore 0:
  11.6 63.3 all-gather.3
  144.3 56.3 all-gather.5
  356.9 139.4 reduce-scatter.16
  499.8 53.2 all-gather.7
  826.5 135.9 reduce-scatter.18
  964.7 131.0 reduce-scatter.12
  1098.0 131.1 reduce-scatter.8
  1231.6 138.3 reduce-scatter.14
  1372.4 144.1 reduce-scatter.10
where the time goes:
time: 1540 us; the launch traced here: 1530 us
  waiting for transfers between devices  866 us (56%)
  matrix products  222 us (14%)
  local copies, waits for them, and re-layouts  138 us (9%)
  other arithmetic  127 us (8%)
  blocking collectives  125 us (8%)
  starting transfers between devices  31.3 us (2%)
  between operations  15.7 us (1%)
    reduce_scatter x1, waiting for transfers between devices, body(): lax.psum_scatter(grad_memoryw, ('seq', 'grp'), scatter_dimension=1, tiled...  145 us
    reduce_scatter x1, waiting for transfers between devices, body(): lax.psum_scatter(grad_up, ('seq', 'grp'), scatter_dimension=0, tiled=True)  139 us
    reduce_scatter x1, waiting for transfers between devices, body(): lax.psum_scatter(grad_down, ('seq', 'grp'), scatter_dimension=0, tiled=True)  139 us
    reduce_scatter x1, waiting for transfers between devices, body(): lax.psum_scatter(grad_queryw, ('seq', 'grp'), scatter_dimension=0, tiled=...  132 us
    reduce_scatter x1, waiting for transfers between devices, body(): lax.psum_scatter(grad_outw, ('seq', 'grp'), scatter_dimension=0, tiled=True)  132 us
    unnamed x10, waiting for transfers between devices  91.5 us
    all_gather x1, waiting for transfers between devices, body(): lax.all_gather(weight_down.astype(jnp.bfloat16), ('seq', 'grp'), axis=0,...  54.9 us
    dot_general x18, matrix products, masked_scores(): jnp.einsum('azv,lzv->zal', query_tile_rows, key_row_block, preferred_elem...  46.7 us
  transfers between devices with their start and end apart: 17, of which 10 were waited for; matrix products, arithmetic and copies ran while one was open for 19% of the time, Pallas kernels for 0%

commit v1 on v0

--- a/solution.py
+++ b/solution.py
@@ -1,6 +1,10 @@
+import functools
+
 import jax
 import jax.numpy as jnp
 from jax import lax
+from jax.experimental import pallas as pl
+from jax.experimental.pallas import tpu as pltpu
 from jax.sharding import PartitionSpec as P
 
 H = 8
@@ -55,91 +59,524 @@
     return (inward, jnp.sum(upstream * unit_rows, axis=0), jnp.sum(upstream, axis=0))
 
 
-def masked_scores(query_tile_rows, key_row_block, positions):
-    slot_starts = 3 * jnp.arange(key_row_block.shape[0], dtype=jnp.int32)
-    score_matrix = jnp.einsum(
-        "azv,lzv->zal", query_tile_rows, key_row_block, preferred_element_type=jnp.float32
-    ) * query_tile_rows.shape[2] ** (-0.5)
-    visible = slot_starts[None, :] <= positions[:, None]
-    return jnp.where(visible[None], score_matrix, MASKED_SCORE)
-
-
-def attend_forward(queries, key_row_block, value_row_block, anchor, block_rows):
-    block_count = queries.shape[0] // block_rows
-    offsets = block_rows * jnp.arange(block_count, dtype=jnp.int32)
-
-    def attend_block(inputs):
-        query_tile_rows, offset_rows = inputs
-        score_matrix = masked_scores(
-            query_tile_rows,
-            key_row_block,
-            anchor + offset_rows + jnp.arange(block_rows, dtype=jnp.int32),
-        )
-        highest = jnp.max(score_matrix, axis=-1, keepdims=True)
-        exponent = jnp.exp(score_matrix - highest)
-        summed = jnp.sum(exponent, axis=-1, keepdims=True)
-        reduced_weights = (exponent / summed).astype(jnp.bfloat16)
-        mixed = jnp.einsum(
-            "yup,pyb->uyb", reduced_weights, value_row_block, preferred_element_type=jnp.float32
-        )
-        return (mixed, (highest + jnp.log(summed))[..., 0])
-
-    blocks_in = queries.reshape(block_count, block_rows, queries.shape[1], queries.shape[2])
-    mixed, logsum = lax.map(attend_block, (blocks_in, offsets))
-    return (mixed.reshape(queries.shape), logsum)
-
-
-def attend_backward(queries, key_row_block, value_row_block, upstream, logsum, anchor, block_rows):
-    block_count = queries.shape[0] // block_rows
-    offsets = block_rows * jnp.arange(block_count, dtype=jnp.int32)
-    scale_factor = queries.shape[2] ** (-0.5)
-
-    def attend_back(carry, inputs):
-        grad_keys, grad_values = carry
-        query_tile_rows, incoming_gradient_rows, logsum_block, offset_rows = inputs
-        score_matrix = masked_scores(
-            query_tile_rows,
-            key_row_block,
-            anchor + offset_rows + jnp.arange(block_rows, dtype=jnp.int32),
-        )
-        weights_soft = jnp.exp(score_matrix - logsum_block[..., None])
-        grad_weights = jnp.einsum(
-            "azv,lzv->zal",
-            incoming_gradient_rows,
-            value_row_block,
-            preferred_element_type=jnp.float32,
-        )
-        centre = jnp.sum(weights_soft * grad_weights, axis=-1, keepdims=True)
-        score_gradient = (weights_soft * (grad_weights - centre)).astype(jnp.bfloat16)
-        grad_query = (
-            jnp.einsum(
-                "yup,pyb->uyb", score_gradient, key_row_block, preferred_element_type=jnp.float32
-            )
-            * scale_factor
-        )
-        grad_keys = (
-            grad_keys
-            + jnp.einsum(
-                "xof,oxa->fxa", score_gradient, query_tile_rows, preferred_element_type=jnp.float32
-            )
-            * scale_factor
-        )
-        grad_values = grad_values + jnp.einsum(
-            "xof,oxa->fxa",
-            weights_soft.astype(jnp.bfloat16),
-            incoming_gradient_rows,
-            preferred_element_type=jnp.float32,
-        )
-        return ((grad_keys, grad_values), grad_query)
-
-    shape_blocks = (block_count, block_rows, queries.shape[1], queries.shape[2])
-    zeros_init = jnp.zeros(key_row_block.shape, jnp.float32)
-    (grad_keys, grad_values), grad_query = lax.scan(
-        attend_back,
-        (zeros_init, zeros_init),
-        (queries.reshape(shape_blocks), upstream.reshape(shape_blocks), logsum, offsets),
-    )
-    return (grad_query.reshape(queries.shape), grad_keys, grad_values)
+MESH = pl.DeviceIdType.MESH
+ROWS = 16
+VMEM_LIMIT = 60 * 1024 * 1024
+
+
+def in_vmem(count):
+    return [pl.BlockSpec(memory_space=pltpu.VMEM)] * count
+
+
+class Place:
+    def __init__(self, depth):
+        seq, grp = lax.axis_index("seq"), lax.axis_index("grp")
+        self.depth = depth
+        self.y, self.x = lax.div(seq, 2), lax.rem(seq, 2)
+        self.z, self.c = lax.div(grp, 2), lax.rem(grp, 2)
+        self.seq, self.grp = seq, grp
+
+    def over_x(self):
+        return {"seq": 2 * self.y + 1 - self.x}
+
+    def over_y(self):
+        return {"seq": 2 * (1 - self.y) + self.x}
+
+    def over_core(self):
+        return {"grp": 2 * self.z + 1 - self.c}
+
+    def z_of(self, step):
+        return lax.rem(self.z + step, self.depth)
+
+    def over_z(self, step):
+        return {"grp": 2 * self.z_of(step) + self.c}
+
+    def peers(self):
+        return [self.over_x(), self.over_y(), self.over_core()] + [
+            self.over_z(step) for step in range(1, self.depth)
+        ]
+
+    def greet(self, peers):
+        barrier = pltpu.get_barrier_semaphore()
+        for peer in peers:
+            pl.semaphore_signal(barrier, inc=1, device_id=peer, device_id_type=MESH)
+        pl.semaphore_wait(barrier, len(peers))
+
+
+def copy_to(source, target, sems, index, peer):
+    send, recv = sems
+    return pltpu.make_async_remote_copy(
+        src_ref=source,
+        dst_ref=target,
+        send_sem=send.at[index],
+        recv_sem=recv.at[index],
+        device_id=peer,
+        device_id_type=MESH,
+    )
+
+
+class Gather:
+    def __init__(self, place, view, sems, base, x_first):
+        self.at, self.view, self.sems, self.base, self.x_first = place, view, sems, base, x_first
+
+    def copy(self, region, slot, peer):
+        made = copy_to(region, region, self.sems, self.base + slot, peer)
+        made.start()
+        return made
+
+    def stage0(self):
+        p = self.at
+        own = self.view(p.y, p.x, p.z, p.c)
+        self.open = [self.copy(own, step - 1, p.over_z(step)) for step in range(1, p.depth)]
+
+    def stage1(self):
+        p = self.at
+        for made in self.open:
+            made.wait()
+        region = self.view(p.y, p.x, slice(None), p.c)
+        self.open = [self.copy(region, p.depth - 1, p.over_x() if self.x_first else p.over_y())]
+
+    def stage2(self):
+        p = self.at
+        self.open[0].wait()
+        if self.x_first:
+            region, peer = self.view(p.y, slice(None), slice(None), p.c), p.over_y()
+        else:
+            region, peer = self.view(slice(None), p.x, slice(None), p.c), p.over_x()
+        self.open = [self.copy(region, p.depth, peer), self.copy(region, p.depth + 1, p.over_core())]
+
+    def stage3(self):
+        p = self.at
+        self.open[0].wait()
+        if self.x_first:
+            region = self.view(1 - p.y, slice(None), slice(None), p.c)
+        else:
+            region = self.view(slice(None), 1 - p.x, slice(None), p.c)
+        self.open = [self.open[1], self.copy(region, p.depth + 2, p.over_core())]
+
+    def stage4(self):
+        for made in self.open:
+            made.wait()
+
+
+def gather_slots(depth):
+    return depth + 3
+
+
+def gather_kernel(depth, wq, wm, wo, wu, wd, vec, stack, down, vectors, tiles, send, recv):
+    p = Place(depth)
+    own = (p.y, p.x, p.z, p.c)
+    low = jnp.bfloat16
+    width = stack.shape[-1]
+    stack[(0,) + own] = wq[...].astype(low)
+    for tap in range(3):
+        for half in range(2):
+            stack[(1 + 2 * tap + half,) + own] = wm[tap, :, half * width : (half + 1) * width].astype(low)
+    stack[(7,) + own] = wo[...].astype(low)
+    for part in range(4):
+        stack[(8 + part,) + own] = wu[:, part * width : (part + 1) * width].astype(low)
+    down[own] = wd[...].astype(low)
+    tiles[own] = vec[...].astype(low)
+    p.greet(p.peers())
+    views = [lambda *i: tiles.at[i]]
+    views += [functools.partial(lambda j, *i: stack.at[(j,) + i], j) for j in range(12)]
+    views += [
+        functools.partial(lambda k, *i: down.at[i + (pl.ds(k * ROWS, ROWS),)], k)
+        for k in range(down.shape[4] // ROWS)
+    ]
+    views = [
+        functools.partial(lambda v, *i: v(*[pl.ds(0, n) if isinstance(k, slice) else k for k, n in zip(i, (2, 2, depth, 2))]), v)
+        for v in views
+    ]
+    slots = gather_slots(depth)
+    pieces = [
+        Gather(p, view, (send, recv), slots * k, k % 2 == 0) for k, view in enumerate(views)
+    ]
+    for stage in ("stage0", "stage1", "stage2", "stage3", "stage4"):
+        for piece in pieces:
+            getattr(piece, stage)()
+    lanes = tiles.shape[-1]
+    for y in range(2):
+        for x in range(2):
+            total = jnp.zeros(tiles.shape[-2:], jnp.float32)
+            for z in range(depth):
+                for c in range(2):
+                    total += tiles[y, x, z, c].astype(jnp.float32)
+            s = 2 * y + x
+            vectors[:, s * lanes : (s + 1) * lanes] = total
+
+
+def gather_plain(params):
+    wq, wm, wo, wu, wd, vec = [member.astype(jnp.bfloat16) for member in params]
+    axes = ("seq", "grp")
+    return (
+        lax.all_gather(wq, axes, axis=0, tiled=True),
+        lax.all_gather(wm, axes, axis=1, tiled=True),
+        lax.all_gather(wo, axes, axis=0, tiled=True),
+        lax.all_gather(wu, axes, axis=0, tiled=True),
+        lax.all_gather(wd, axes, axis=0, tiled=True),
+        lax.all_gather(vec, axes, axis=1, tiled=True).astype(jnp.float32),
+    )
+
+
+def gather_parameters(params):
+    wq, wm, wo, wu, wd, vec = params
+    groups = lax.axis_size("grp")
+    depth = groups // 2
+    rows, width = wq.shape
+    lanes = vec.shape[1] * groups
+    tile = lax.dynamic_update_slice(
+        jnp.zeros((ROWS, lanes), jnp.float32), vec, (0, vec.shape[1] * lax.axis_index("grp"))
+    )
+    low = jnp.bfloat16
+    pieces = 13 + wd.shape[0] // ROWS
+    sems = pltpu.SemaphoreType.DMA((pieces * gather_slots(depth),))
+    stack, down, vectors = pl.pallas_call(
+        functools.partial(gather_kernel, depth),
+        out_shape=(
+            jax.ShapeDtypeStruct((12, 2, 2, depth, 2, rows, width), low),
+            jax.ShapeDtypeStruct((2, 2, depth, 2) + wd.shape, low),
+            jax.ShapeDtypeStruct((ROWS, 4 * lanes), jnp.float32),
+        ),
+        in_specs=in_vmem(6),
+        out_specs=in_vmem(3),
+        scratch_shapes=[pltpu.VMEM((2, 2, depth, 2, ROWS, lanes), low), sems, sems],
+        compiler_params=pltpu.CompilerParams(
+            collective_id=0, has_side_effects=True, vmem_limit_bytes=VMEM_LIMIT
+        ),
+    )(wq, wm, wo, wu, wd, tile)
+    full = stack.reshape(12, width, width)
+    memory = jnp.stack([jnp.concatenate([full[1 + 2 * k], full[2 + 2 * k]], axis=1) for k in range(3)])
+    up = jnp.concatenate([full[8 + k] for k in range(4)], axis=1)
+    return (full[0], memory, full[7], up, down.reshape(-1, width), vectors[:9])
+
+
+class Scatter:
+    def __init__(self, place, view, out, scratch, sems, base, number, x_first):
+        self.at, self.view, self.out, self.sems, self.base = place, view, out, sems, base
+        self.bufs = [ref.at[number] for ref in scratch]
+        self.x_first = x_first
+
+    def copy(self, source, target, slot, peer):
+        made = copy_to(source, target, self.sems, self.base + slot, peer)
+        made.start()
+        return made
+
+    def stage0(self):
+        p = self.at
+        give, get = self.bufs[0], self.bufs[1]
+        for y in range(2):
+            for x in range(2):
+                give[y, x] = self.view(y, x, pl.ds(0, p.depth), 1 - p.c)[...].astype(jnp.bfloat16)
+        self.open = [self.copy(give, get, 0, p.over_core())]
+
+    def part(self, other, kept):
+        p = self.at
+        y, x = (other, kept) if self.x_first else (kept, other)
+        return self.view(y, x, pl.ds(0, p.depth), p.c)[...] + self.bufs[1][y, x].astype(jnp.float32)
+
+    def stage1(self):
+        p = self.at
+        _, _, give, get, keep = self.bufs[:5]
+        self.open[0].wait()
+        mine, peer = (p.x, p.over_x()) if self.x_first else (p.y, p.over_y())
+        for other in range(2):
+            give[other] = self.part(other, 1 - mine).astype(jnp.bfloat16)
+        self.open = [self.copy(give, get, 1, peer)]
+        for other in range(2):
+            keep[other] = self.part(other, mine)
+
+    def stage2(self):
+        p = self.at
+        _, _, _, get, keep, give_two, get_two, _, _ = self.bufs
+        self.open[0].wait()
+        mine, peer = (p.y, p.over_y()) if self.x_first else (p.x, p.over_x())
+        give_two[...] = (keep[1 - mine] + get[1 - mine].astype(jnp.float32)).astype(jnp.bfloat16)
+        self.open = [self.copy(give_two, get_two, 2, peer)]
+        keep[mine] = keep[mine] + get[mine].astype(jnp.float32)
+
+    def stage3(self):
+        p = self.at
+        keep, _, get_two, give_z, get_z = self.bufs[4:]
+        self.open[0].wait()
+        mine = p.y if self.x_first else p.x
+        total = keep[mine] + get_two[...].astype(jnp.float32)
+        keep[mine] = total
+        give_z[...] = total.astype(jnp.bfloat16)
+        self.open = [
+            self.copy(give_z.at[p.z_of(step)], get_z.at[step - 1], 2 + step, p.over_z(step))
+            for step in range(1, p.depth)
+        ]
+
+    def stage4(self):
+        p = self.at
+        keep, _, _, _, get_z = self.bufs[4:]
+        mine = p.y if self.x_first else p.x
+        for made in self.open:
+            made.wait()
+        total = keep[mine, p.z]
+        for step in range(1, p.depth):
+            total = total + get_z[step - 1].astype(jnp.float32)
+        self.out(total)
+
+
+def scatter_slots(depth):
+    return depth + 2
+
+
+def scatter_scratch(count, depth, width):
+    low, wide = jnp.bfloat16, jnp.float32
+    return [
+        pltpu.VMEM((count, 2, 2, depth, ROWS, width), low),
+        pltpu.VMEM((count, 2, 2, depth, ROWS, width), low),
+        pltpu.VMEM((count, 2, depth, ROWS, width), low),
+        pltpu.VMEM((count, 2, depth, ROWS, width), low),
+        pltpu.VMEM((count, 2, depth, ROWS, width), wide),
+        pltpu.VMEM((count, depth, ROWS, width), low),
+        pltpu.VMEM((count, depth, ROWS, width), low),
+        pltpu.VMEM((count, depth, ROWS, width), low),
+        pltpu.VMEM((count, depth - 1, ROWS, width), low),
+    ]
+
+
+class SumAll:
+    def __init__(self, place, out, give, get, sems, base):
+        self.at, self.out, self.give, self.get, self.sems, self.base = place, out, give, get, sems, base
+
+    def send(self, slot, peer):
+        made = copy_to(self.give.at[min(slot, 3)], self.get.at[slot], self.sems, self.base + slot, peer)
+        made.start()
+        return made
+
+    def stage(self, number):
+        p = self.at
+        if number:
+            self.open[0].wait()
+            self.give[number] = self.give[number - 1] + self.get[number - 1]
+        if number < 3:
+            self.open = [self.send(number, (p.over_core(), p.over_x(), p.over_y())[number])]
+        else:
+            self.open = [self.send(2 + step, p.over_z(step)) for step in range(1, p.depth)]
+
+    def finish(self):
+        total = self.give[3]
+        for made in self.open:
+            made.wait()
+        for step in range(1, self.at.depth):
+            total = total + self.get[2 + step]
+        self.out[...] = total
+
+
+def scatter_kernel(depth, stack, down, vec, out_stack, out_down, out_vec, *scratch):
+    p = Place(depth)
+    bufs, (give, get, send, recv) = scratch[:-4], scratch[-4:]
+    count = 12 + down.shape[4] // ROWS
+    slots = scatter_slots(depth)
+    p.greet(p.peers())
+
+    def to_stack(j, value):
+        out_stack[j] = value
+
+    def to_down(k, value):
+        out_down[k * ROWS : (k + 1) * ROWS] = value
+
+    pieces = []
+    for j in range(count):
+        if j < 12:
+            view = functools.partial(lambda j, *i: stack.at[(j,) + i], j)
+            out = functools.partial(to_stack, j)
+        else:
+            view = functools.partial(lambda k, *i: down.at[i + (pl.ds(k * ROWS, ROWS),)], j - 12)
+            out = functools.partial(to_down, j - 12)
+        pieces.append(Scatter(p, view, out, bufs, (send, recv), slots * j, j, j % 2 == 0))
+    small = SumAll(p, out_vec, give, get, (send, recv), slots * count)
+    give[0] = vec[...]
+    for number in range(4):
+        small.stage(number)
+        for piece in pieces:
+            getattr(piece, f"stage{number}")()
+    for piece in pieces:
+        piece.stage4()
+    small.finish()
+
+
+def scatter_plain(grads):
+    axes = ("seq", "grp")
+    return tuple(
+        lax.psum_scatter(member, axes, scatter_dimension=dim, tiled=True)
+        for member, dim in zip(grads, (0, 1, 0, 0, 0, 1))
+    )
+
+
+def scatter_gradients(grads):
+    gq, gm, go, gu, gd, gv = grads
+    groups = lax.axis_size("grp")
+    depth = groups // 2
+    width = gq.shape[1]
+    devices = 4 * groups
+    shape = (2, 2, depth, 2)
+    own_down = gd.shape[0] // devices
+    stack = jnp.stack(
+        [gq]
+        + [gm[k, :, h * width : (h + 1) * width] for k in range(3) for h in range(2)]
+        + [go]
+        + [gu[:, k * width : (k + 1) * width] for k in range(4)]
+    ).reshape((12,) + shape + (ROWS, width))
+    count = 12 + own_down // ROWS
+    sems = pltpu.SemaphoreType.DMA((count * scatter_slots(depth) + depth + 2,))
+    vec = jnp.pad(gv, ((0, ROWS - gv.shape[0]), (0, 0)))
+    wide = jnp.float32
+    out_stack, out_down, out_vec = pl.pallas_call(
+        functools.partial(scatter_kernel, depth),
+        out_shape=(
+            jax.ShapeDtypeStruct((12, ROWS, width), wide),
+            jax.ShapeDtypeStruct((own_down, width), wide),
+            jax.ShapeDtypeStruct(vec.shape, wide),
+        ),
+        in_specs=in_vmem(3),
+        out_specs=in_vmem(3),
+        scratch_shapes=scatter_scratch(count, depth, width)
+        + [
+            pltpu.VMEM((4,) + vec.shape, wide),
+            pltpu.VMEM((depth + 2,) + vec.shape, wide),
+            sems,
+            sems,
+        ],
+        compiler_params=pltpu.CompilerParams(
+            collective_id=1, has_side_effects=True, vmem_limit_bytes=VMEM_LIMIT
+        ),
+    )(stack, gd.reshape(shape + (own_down, width)), vec)
+    share = gv.shape[1] // devices
+    index = lax.axis_index("seq") * groups + lax.axis_index("grp")
+    return (
+        out_stack[0],
+        jnp.stack([jnp.concatenate([out_stack[1 + 2 * k], out_stack[2 + 2 * k]], axis=1) for k in range(3)]),
+        out_stack[7],
+        jnp.concatenate([out_stack[8 + k] for k in range(4)], axis=1),
+        out_down,
+        lax.dynamic_slice(out_vec, (0, index * share), (gv.shape[0], share)),
+    )
+
+
+STRIP = 256
+NT = (((1,), (1,)), ((), ()))
+
+
+def head_only(values, head, size):
+    lane = lax.broadcasted_iota(jnp.int32, values.shape, 1)
+    keep = jnp.logical_and(lane >= head * size, lane < (head + 1) * size)
+    return jnp.where(keep, values, jnp.zeros_like(values))
+
+
+def hide_future(scores, first_slot, first_row):
+    slot = lax.broadcasted_iota(jnp.int32, scores.shape, 0) + first_slot
+    row = lax.broadcasted_iota(jnp.int32, scores.shape, 1) + first_row
+    return jnp.where(3 * slot <= row, scores, MASKED_SCORE)
+
+
+def strip_scores(keys, queries, seen, first_row):
+    if seen == STRIP:
+        return hide_future(lax.dot_general(keys[0:seen, :], queries, NT, preferred_element_type=jnp.float32), 0, first_row)
+    whole = seen - STRIP
+    past = lax.dot_general(keys[0:whole, :], queries, NT, preferred_element_type=jnp.float32)
+    last = lax.dot_general(keys[whole:seen, :], queries, NT, preferred_element_type=jnp.float32)
+    return jnp.concatenate([past, hide_future(last, whole, first_row)], axis=0)
+
+
+def forward_kernel(heads, q_ref, k_ref, v_ref, o_ref, lse_ref, vt_ref):
+    lanes = q_ref.shape[1]
+    size = lanes // heads
+    vt_ref[...] = v_ref[...].T
+    for block in range(q_ref.shape[0] // (3 * STRIP)):
+        seen = STRIP * (block + 1)
+
+        @pl.loop(0, 3)
+        def _(part):
+            first = pl.multiple_of((3 * block + part) * STRIP, STRIP)
+            rows = pl.ds(first, STRIP)
+            queries = q_ref[rows, :] * jnp.bfloat16(size ** (-0.5))
+            mixed = []
+            for head in range(heads):
+                scores = strip_scores(k_ref, head_only(queries, head, size), seen, first)
+                highest = jnp.max(scores, axis=0, keepdims=True)
+                exponent = jnp.exp(scores - highest)
+                summed = jnp.sum(exponent, axis=0, keepdims=True)
+                out = jnp.dot(
+                    vt_ref[head * size : (head + 1) * size, 0:seen],
+                    exponent.astype(jnp.bfloat16),
+                    preferred_element_type=jnp.float32,
+                )
+                mixed.append(out / summed)
+                lse_ref[head : head + 1, rows] = highest + jnp.log(summed)
+            o_ref[rows, :] = jnp.concatenate(mixed, axis=0).T.astype(jnp.bfloat16)
+
+
+def backward_kernel(heads, q_ref, k_ref, v_ref, do_ref, o_ref, lse_ref, dq_ref, dk_ref, dv_ref, kt_ref):
+    lanes = q_ref.shape[1]
+    size = lanes // heads
+    scale = size ** (-0.5)
+    low = jnp.bfloat16
+    kt_ref[...] = k_ref[...].T
+    dk_ref[...] = jnp.zeros_like(dk_ref)
+    dv_ref[...] = jnp.zeros_like(dv_ref)
+    for block in range(q_ref.shape[0] // (3 * STRIP)):
+        seen = STRIP * (block + 1)
+
+        @pl.loop(0, 3)
+        def _(part):
+            first = pl.multiple_of((3 * block + part) * STRIP, STRIP)
+            rows = pl.ds(first, STRIP)
+            queries = q_ref[rows, :] * low(scale)
+            incoming = do_ref[rows, :]
+            centre = (incoming.astype(jnp.float32) * o_ref[rows, :].astype(jnp.float32)).T
+            grads = []
+            for head in range(heads):
+                own_q = head_only(queries, head, size)
+                own_do = head_only(incoming, head, size)
+                scores = strip_scores(k_ref, own_q, seen, first)
+                weights = jnp.exp(scores - lse_ref[head : head + 1, rows])
+                back = lax.dot_general(v_ref[0:seen, :], own_do, NT, preferred_element_type=jnp.float32)
+                middle = jnp.sum(centre[head * size : (head + 1) * size], axis=0, keepdims=True)
+                slope = (weights * (back - middle)).astype(low)
+                dv_ref[0:seen, :] += jnp.dot(weights.astype(low), own_do, preferred_element_type=jnp.float32)
+                dk_ref[0:seen, :] += jnp.dot(slope, own_q, preferred_element_type=jnp.float32)
+                grads.append(
+                    jnp.dot(kt_ref[head * size : (head + 1) * size, 0:seen], slope, preferred_element_type=jnp.float32)
+                )
+            dq_ref[rows, :] = (jnp.concatenate(grads, axis=0) * scale).T.astype(low)
+
+
+def attend_forward(queries, keys, values):
+    rows, lanes = queries.shape
+    heads = H * lanes // (lax.axis_size("seq") * lanes)
+    return pl.pallas_call(
+        functools.partial(forward_kernel, heads),
+        out_shape=(
+            jax.ShapeDtypeStruct((rows, lanes), jnp.bfloat16),
+            jax.ShapeDtypeStruct((heads, rows), jnp.float32),
+        ),
+        in_specs=in_vmem(3),
+        out_specs=in_vmem(2),
+        scratch_shapes=[pltpu.VMEM((lanes, keys.shape[0]), jnp.bfloat16)],
+        compiler_params=pltpu.CompilerParams(vmem_limit_bytes=VMEM_LIMIT),
+    )(queries, keys, values)
+
+
+def attend_backward(queries, keys, values, upstream, mixed, logsum):
+    rows, lanes = queries.shape
+    heads = logsum.shape[0]
+    return pl.pallas_call(
+        functools.partial(backward_kernel, heads),
+        out_shape=(
+            jax.ShapeDtypeStruct((rows, lanes), jnp.bfloat16),
+            jax.ShapeDtypeStruct(keys.shape, jnp.float32),
+            jax.ShapeDtypeStruct(keys.shape, jnp.float32),
+        ),
+        in_specs=in_vmem(6),
+        out_specs=in_vmem(3),
+        scratch_shapes=[pltpu.VMEM((lanes, keys.shape[0]), jnp.bfloat16)],
+        compiler_params=pltpu.CompilerParams(vmem_limit_bytes=VMEM_LIMIT),
+    )(queries, keys, values, upstream, mixed, logsum)
 
 
 def adamw(weight, gradient, moment, square, step_rate):
@@ -178,16 +615,10 @@
     second_down,
     second_vectors,
 ):
-    gathered = (
-        lax.all_gather(weight_query.astype(jnp.bfloat16), ("seq", "grp"), axis=0, tiled=True),
-        lax.all_gather(weight_memory.astype(jnp.bfloat16), ("seq", "grp"), axis=1, tiled=True),
-        lax.all_gather(weight_out.astype(jnp.bfloat16), ("seq", "grp"), axis=0, tiled=True),
-        lax.all_gather(weight_up.astype(jnp.bfloat16), ("seq", "grp"), axis=0, tiled=True),
-        lax.all_gather(weight_down.astype(jnp.bfloat16), ("seq", "grp"), axis=0, tiled=True),
-        lax.all_gather(vectors.astype(jnp.bfloat16), ("seq", "grp"), axis=1, tiled=True),
-    )
-    query_w, memory_w, out_w, up_w, down_w, vector_low = gathered
-    vector_rows = vector_low.astype(jnp.float32)
+    fast = weight_query.shape[0] % 16 == 0 and lax.axis_size("seq") == 4
+    params = (weight_query, weight_memory, weight_out, weight_up, weight_down, vectors)
+    gathered = gather_parameters(params) if fast else gather_plain(params)
+    query_w, memory_w, out_w, up_w, down_w, vector_rows = gathered
     model_width = query_w.shape[0]
     hidden_units = up_w.shape[1]
     head_size = model_width // H
@@ -224,12 +655,11 @@
     )
     total_rows = head_queries.shape[0]
     total_slots = head_memory.shape[0]
-    query_heads = head_queries.reshape(total_rows, local_heads, head_size)
-    key_heads = head_memory[:, 0].reshape(total_slots, local_heads, head_size)
-    value_heads = head_memory[:, 1].reshape(total_slots, local_heads, head_size)
-    block_rows = min(512, total_rows)
-    mixed, logsum = attend_forward(query_heads, key_heads, value_heads, 0, block_rows)
-    mixed_low = mixed.astype(jnp.bfloat16).reshape(total_rows, 1, share_width)
+    query_heads = head_queries.reshape(total_rows, share_width)
+    key_heads = head_memory[:, 0].reshape(total_slots, share_width)
+    value_heads = head_memory[:, 1].reshape(total_slots, share_width)
+    mixed, logsum = attend_forward(query_heads, key_heads, value_heads)
+    mixed_low = mixed.reshape(total_rows, 1, share_width)
     attended = lax.all_to_all(mixed_low, "seq", split_axis=0, concat_axis=1, tiled=True).reshape(
         local_rows, model_width
     )
@@ -263,9 +693,9 @@
         split_axis=2,
         concat_axis=0,
         tiled=True,
-    ).reshape(total_rows, local_heads, head_size)
+    ).reshape(total_rows, share_width)
     grad_q, grad_k, grad_v = attend_backward(
-        query_heads, key_heads, value_heads, grad_heads, logsum, 0, block_rows
+        query_heads, key_heads, value_heads, grad_heads, mixed, logsum
     )
     packed = (
         jnp.stack([grad_k, grad_v], axis=1)
@@ -309,14 +739,8 @@
         ],
         axis=0,
     )
-    reduced = (
-        lax.psum_scatter(grad_queryw, ("seq", "grp"), scatter_dimension=0, tiled=True),
-        lax.psum_scatter(grad_memoryw, ("seq", "grp"), scatter_dimension=1, tiled=True),
-        lax.psum_scatter(grad_outw, ("seq", "grp"), scatter_dimension=0, tiled=True),
-        lax.psum_scatter(grad_up, ("seq", "grp"), scatter_dimension=0, tiled=True),
-        lax.psum_scatter(grad_down, ("seq", "grp"), scatter_dimension=0, tiled=True),
-        lax.psum_scatter(grad_vector_rows, ("seq", "grp"), scatter_dimension=1, tiled=True),
-    )
+    grads = (grad_queryw, grad_memoryw, grad_outw, grad_up, grad_down, grad_vector_rows)
+    reduced = scatter_gradients(grads) if fast else scatter_plain(grads)
     new_query = adamw(weight_query, reduced[0], first_query, second_query, LEARNING_RATES[0])
     new_memory = adamw(weight_memory, reduced[1], first_memory, second_memory, LEARNING_RATES[1])
     new_out = adamw(weight_out, reduced[2], first_out, second_out, LEARNING_RATES[2])

time: 1540 us -> 470 us (0.31)
  waiting for transfers between devices: 866 us -> 34.7 us
  Pallas kernels: 0 us -> 186 us
  matrix products: 222 us -> 76.9 us
  blocking collectives: 125 us -> 0 us
  other arithmetic: 127 us -> 26.4 us
  local copies, waits for them, and re-layouts: 138 us -> 107 us
    reduce_scatter x5 -> x0, waiting for transfers between devices: 687 us -> none  [the longest x1 145 us: body(): lax.psum_scatter(grad_memoryw, ('seq', 'grp'), scatter_dimension=1, tiled...]
    pallas_call x0 -> x4, Pallas kernels: none -> 186 us  [the longest x1 68.1 us: scatter_gradients(): pl.pallas_call(functools.partial(scatter_kernel, depth), out_shape=(jax.S...]
    dot_general x63 -> x0, matrix products: 146 us -> none  [the longest x18 46.7 us: masked_scores(): jnp.einsum('azv,lzv->zal', query_tile_rows, key_row_block, preferred_elem...]
    all_gather x3 -> x0, blocking collectives: 125 us -> none  [the longest x1 43.9 us: body(): lax.all_gather(vectors.astype(jnp.bfloat16), ('seq', 'grp'), axis=1, tile...]
    unnamed x10 -> x0, waiting for transfers between devices: 91.5 us -> none
    convert_element_type x16 -> x0, other arithmetic: 59.8 us -> none  [the longest x1 26.2 us: body(): mixed_low = mixed.astype(jnp.bfloat16).reshape(total_rows, 1, share_width)]
    all_gather x3 -> x0, waiting for transfers between devices: 55 us -> none  [the longest x1 54.9 us: body(): lax.all_gather(weight_down.astype(jnp.bfloat16), ('seq', 'grp'), axis=0,...]
    convert_element_type x5 -> x1, local copies, waits for them, and re-layouts: 29.6 us -> 6.73 us  [body(): activated_low = activated.astype(jnp.bfloat16)]
  transfers between devices with their start and end apart: 17 -> 8, of which waited for: 10 -> 4; matrix products, arithmetic and copies ran while one was open for 19% -> 15% of each run, Pallas kernels for 0% -> 0%
where the time goes in v1:
time: 470 us; the launch traced here: 461 us
  Pallas kernels  186 us (40%)
  local copies, waits for them, and re-layouts  107 us (23%)
  matrix products  76.9 us (16%)
  waiting for transfers between devices  34.7 us (7%)
  starting transfers between devices  28.4 us (6%)
  other arithmetic  26.4 us (6%)
    pallas_call x1, Pallas kernels, scatter_gradients(): pl.pallas_call(functools.partial(scatter_kernel, depth), out_shape=(jax.S...  68.1 us
    pallas_call x1, Pallas kernels, gather_parameters(): pl.pallas_call(functools.partial(gather_kernel, depth), out_shape=(jax.Sh...  63 us
    unnamed x167, local copies, waits for them, and re-layouts  40.5 us
    dot_general x5, matrix products, against(): lax.dot_general(left, right, (((1,), (1,)), ((), ())), preferred_element_...  29.6 us
    pallas_call x1, Pallas kernels, attend_backward(): pl.pallas_call(functools.partial(backward_kernel, heads), out_shape=(jax....  29.1 us
    dot_general x5, matrix products, matmul(): return jnp.dot(left, right, preferred_element_type=jnp.float32)  26.7 us
    pallas_call x1, Pallas kernels, attend_forward(): pl.pallas_call(functools.partial(forward_kernel, heads), out_shape=(jax.S...  25.5 us
    dot_general x5, matrix products, over_rows(): lax.dot_general(left, right, (((0,), (0,)), ((), ())), preferred_element_...  20.7 us
  transfers between devices with their start and end apart: 8, of which 4 were waited for; matrix products, arithmetic and copies ran while one was open for 15% of the time, Pallas kernels for 0%

profile of v1, /device:TPU:0, one launch (start us, length us, event | category | flops | bytes accessed | tf_op | source)
XLA Modules:
  0.0 461.5 jit_solution(5072179732552136077)
XLA Ops:
  4.0 63.0 %shard_map.404 = (bf16[12,2,2,4,2,16,512]{6,5,4,3,2,1,0:T(8,128)(2,1)}, bf16[2,2,4,2,64,512]{5,4,3,2,1,0:T(8,128)(2,1)}, f32[16,512]{1,0:T(8,128)}) custom-call(f32[16,512]{1,0:T(8,128)} %wq.1, f32[3,16,1024]{2,1,0:T(8,128)} %wm.1, f32[16,512]{1,0:T(8,128)} %wo.1, f32[16,2048]{1,0:T(8,128)} %wu.1, f32[64,512]{1,0:T(8,128)} %wd.1, f32[16,128]{1,0:T(8,128)} %copy-done.43), custom_call_target="tpu_custom_call" | custom-call | tf_op jit(solution)/shard_map/pallas_call | solution.py:234
  72.1 5.0 %fusion.94 = (bf16[1,2,2,4,2,16,512]{6,5,4,3,2,1,0:T(8,128)(2,1)}, bf16[1,2,2,4,2,16,512]{6,5,4,3,2,1,0:T(8,128)(2,1)}, bf16[1,2,2,4,2,16,512]{6,5,4,3,2,1,0:T(8...) fusion(bf16[12,2,2,4,2,16,512]{6,5,4,3,2,1,0:T(8,128)(2,1)} %ge, ...), kind=kLoop, calls=%fused_computation.171 | loop fusion | bytes 12582912 | tf_op jit(solution)/shard_map/slice | solution.py:250
  83.8 4.2 convolution_convert_fusion.2
  91.0 3.5 all-to-all-start.1
  100.3 5.5 %all-to-all-done.1 = bf16[384,2,4,128]{3,0,1,2:T(8,128)(2,1)S(1)} async-done(((bf16[384,2,4,128]{3,0,1,2:T(8,128)(2,1)}), bf16[384,2,4,128]{3,0,1,2:T(8,128)(2,1)S(1)}, u32[]{:S(2)}, u32[]{:S(2)}) %all-to-all-start.1) | async-done | bytes 786464 | tf_op jit(solution)/shard_map/all_to_all | solution.py:648
  106.7 3.7 all-to-all-start
  112.5 12.5 %all-to-all-done = bf16[1152,1,4,128]{3,0,1,2:T(8,128)(2,1)S(1)} async-done(((bf16[1152,1,4,128]{3,0,1,2:T(8,128)(2,1)}), bf16[1152,1,4,128]{3,0,1,2:T(8,128)(2,1)S(1)}, u32[]{:S(2)}, u32[]{:S(2)}) %all-to-all-start) | async-done | bytes 1179680 | tf_op jit(solution)/shard_map/all_to_all | solution.py:641
  126.1 25.5 %shard_map.405 = (bf16[4608,128]{1,0:T(8,128)(2,1)}, f32[2,4608]{1,0:T(2,128)}) custom-call(bf16[4608,128]{1,0:T(8,128)(2,1)} %bitcast.246, bf16[1536,128]{1,0:T(8,128)(2,1)} %get-tuple-element.234.k_ref, bf16[1536,128]{1,0:T(8,128)(2,1)} %get-tuple-element.233.v_ref), custom_call_target="tpu_custom_call" | custom-call | tf_op jit(solution)/shard_map/pallas_call | solution.py:552
  156.6 4.7 %all-to-all-start.2 = ((bf16[4,2,73728]{2,1,0:T(2,128)(2,1)}), bf16[4,2,73728]{2,1,0:T(2,128)(2,1)}, u32[]{:S(2)}, u32[]{:S(2)}) async-start(bf16[4,2,73728]{2,1,0:T(2,128)(2,1)} %reshape.340), calls=%async_computation.2 | async-start | bytes 2359296 | tf_op jit(solution)/shard_map/all_to_all | solution.py:663
  166.7 9.1 %all-to-all-done.2 = bf16[4,2,73728]{2,1,0:T(2,128)(2,1)} async-done(((bf16[4,2,73728]{2,1,0:T(2,128)(2,1)}), bf16[4,2,73728]{2,1,0:T(2,128)(2,1)}, u32[]{:S(2)}, u32[]{:S(2)}) %all-to-all-start.2) | async-done | bytes 1179680 | tf_op jit(solution)/shard_map/all_to_all | solution.py:663
  186.0 8.9 %fusion.14 = (bf16[2048,1152]{0,1:T(8,128)(2,1)}, f32[1152,2048]{1,0:T(8,128)}) fusion(f32[2048]{0:T(1024)S(1)} %bitcast.304, bf16[512,512]{1,0:T(8,128)(2,1)S(1)} %bitcast.287, bf16[512,512]{1,0:T(8,128)(2,1)S(1)} %bitcast.289, bf16[512,512]{1,0:T(8,128)(2,1)S(1)} %bitcast.291, bf16[512,512]{1,0:T(8,128)(2,1)S(1)} %bitcast.285, ...), kind=kOutput, calls=%fused_computation.17 | convolution fusion | flops 2450849792 | bytes 18633728 | tf_op jit(solution)/shard_map/dot_general | solution.py:30
  195.0 6.7 %copy.155 = bf16[2048,1152]{1,0:T(8,128)(2,1)} copy(bf16[2048,1152]{0,1:T(8,128)(2,1)} %get-tuple-element.257) | data formatting | bytes 9437184 | tf_op jit(solution)/shard_map/convert_element_type | solution.py:671
  201.7 9.4 %fusion.26 = bf16[1,1152,512]{1,2,0:T(8,128)(2,1)} fusion(f32[1152,512]{0,1:T(8,128)S(1)} %get-tuple-element.255, bf16[2048,512]{1,0:T(8,128)(2,1)} %bitcast.311, f32[1152,2048]{1,0:T(8,128)} %get-tuple-element.258, f32[512]{0:T(512)} %bitcast.308), kind=kOutput, calls=%fused_computation.41 | convolution fusion | flops 2438922240 | bytes 15075328 | tf_op jit(solution)/shard_map/dot_general | solution.py:30
  211.2 10.9 %convert_reduce_fusion = (f32[2048]{0:T(1024)}, bf16[1152,2048]{1,0:T(8,128)(2,1)}) fusion(f32[1152,2048]{1,0:T(8,128)S(1)} %copy-done.71, bf16[2048,512]{1,0:T(8,128)(2,1)S(1)} %bitcast.312, f32[1152]{0:T(1024)S(1)} %copy-done.51, bf16[1,1152,512]{1,2,0:T(8,128)(2,1)S(1)} %copy-done.5), kind=kOutput, calls=%fused_computation.18 | convolution fusion | flops 2469591040 | bytes 17445376 | tf_op jit(solution)/shard_map/dot_general | solution.py:40
  225.8 7.5 %fusion.98 = (f32[512]{0:T(512)}, f32[1152,512]{1,0:T(8,128)}) fusion(bf16[1152,2048]{1,0:T(8,128)(2,1)} %get-tuple-element.262, bf16[512,512]{1,0:T(8,128)(2,1)} %bitcast.286, bf16[512,512]{1,0:T(8,128)(2,1)} %bitcast.288, bf16[512,512]{1,0:T(8,128)(2,1)} %bitcast.290, bf16[512,512]{1,0:T(8,128)(2,1)} %bitcast.284), kind=kOutput, calls=%fused_computation.175 | convolution fusion | flops 2424897024 | bytes 9177088 | tf_op jit(solution)/shard_map/dot_general | solution.py:40
  233.3 3.1 copy.143
  236.5 3.2 multiply_reduce_fusion
  247.0 4.4 all-to-all-start.3
  251.5 4.9 %fusion.78 = f32[512,2048]{1,0:T(8,128)S(1)} fusion(bf16[1152,2048]{1,0:T(8,128)(2,1)} %get-tuple-element.262, f32[1152,512]{0,1:T(8,128)S(1)} %get-tuple-element.255, f32[512]{0:T(512)} %bitcast.305, f32[512]{0:T(512)} %bitcast.297, f32[1152]{0:T(1024)} %copy-done.41, f32[1152]{0:T(1024)} %copy-done.39), kind=kOutput, calls=%fused_computation.163 | convolution fusion | flops 2418868224 | bytes 11285504 | tf_op jit(solution)/shard_map/dot_general | solution.py:34
  258.5 7.6 %all-to-all-done.3 = bf16[1152,1,4,128]{3,0,1,2:T(8,128)(2,1)} async-done(((bf16[1152,1,4,128]{3,0,1,2:T(8,128)(2,1)}), bf16[1152,1,4,128]{3,0,1,2:T(8,128)(2,1)}, u32[]{:S(2)}, u32[]{:S(2)}) %all-to-all-start.3) | async-done | bytes 1179680 | tf_op jit(solution)/shard_map/all_to_all | solution.py:690
  266.0 29.1 %shard_map.406 = (bf16[4608,128]{1,0:T(8,128)(2,1)}, f32[1536,128]{1,0:T(8,128)}, f32[1536,128]{1,0:T(8,128)}) custom-call(bf16[4608,128]{1,0:T(8,128)(2,1)} %bitcast.247, bf16[1536,128]{1,0:T(8,128)(2,1)} %get-tuple-element.234.k_ref, bf16[1536,128]{1,0:T(8,128)(2,1)} %get-tuple-element.233.v_ref, bf16[4608,128]{1,0:T(8,128)(2,1)} %bitcast.45.do_ref, ...), custom_call_target="tpu_custom_call" | custom-call | tf_op jit(solution)/shard_map/pallas_call | solution.py:568
  297.6 7.5 %copy.147 = bf16[1536,2,1,128]{3,1,2,0:T(2,128)(2,1)} copy(bf16[1536,2,1,128]{3,0,2,1:T(8,128)(2,1)S(1)} %pad_maximum_fusion.3) | data formatting | bytes 1572864 | tf_op jit(solution)/shard_map/stack | solution.py:701
  305.1 3.5 all-to-all-start.5
  308.6 7.0 %fusion.52.down = f32[2,2,4,2,64,512]{5,4,3,2,1,0:T(8,128)} fusion(bf16[2,2,4,2,64,1152]{5,4,3,2,1,0:T(8,128)(2,1)} %bitcast.252, bf16[1,1152,512]{1,2,0:T(8,128)(2,1)S(1)} %copy-done.7, f32[1152]{0:T(1024)S(1)} %copy-done.53), kind=kOutput, calls=%fused_computation.78 | convolution fusion | flops 2417688576 | bytes 10097152 | tf_op jit(solution)/shard_map/dot_general | solution.py:34
  320.1 4.3 all-to-all-start.4
  325.7 4.7 %fusion.99 = f32[384,1536]{1,0:T(8,128)} fusion(bf16[384,1024]{1,0:T(8,128)(2,1)S(1)} %reshape.328, bf16[1536,1024]{1,0:T(8,128)(2,1)} %bitcast.269), kind=kOutput, calls=%fused_computation.176 | convolution fusion | flops 1207959552 | bytes 6291456 | tf_op jit(solution)/shard_map/dot_general | solution.py:40
  337.8 3.3 fusion.100
  345.5 3.3 copy.169
  351.7 5.5 %copy.146 = bf16[1152,1,4,1,128]{4,2,0,3,1:T(4,128)(2,1)S(1)} copy(bf16[1152,1,4,1,128]{4,0,2,3,1:T(8,128)(2,1)S(1)} %bitcast.251) | data formatting | bytes 2359296 | tf_op jit(solution)/shard_map/all_to_all | solution.py:706
  358.6 4.5 fusion.34
  368.6 3.6 fusion.45
  385.3 68.1 %shard_map.407 = (f32[12,16,512]{2,1,0:T(8,128)}, f32[64,512]{1,0:T(8,128)}, f32[16,512]{1,0:T(8,128)}) custom-call(f32[12,2,2,4,2,16,512]{6,5,4,3,2,1,0:T(8,128)} %constant_dynamic-update-slice_fusion.stack, f32[2,2,4,2,64,512]{5,4,3,2,1,0:T(8,128)} %fusion.52.down, f32[16,512]{1,0:T(8,128)} %pad.4.vec), custom_call_target="tpu_custom_call" | custom-call | tf_op jit(solution)/shard_map/pallas_call | solution.py:429
  (239 shorter events, 111.0 us)
Async XLA Ops:
  69.1 10.4 %collective-permute-start = (bf16[2,512]{0,1:T(8,128)(2,1)S(1)}, bf16[2,512]{0,1:T(8,128)(2,1)S(1)}, u32[]{:S(2)}, u32[]{:S(2)}) collective-permute-start(bf16[2,512]{0,1:T(8,128)(2,1)S(1)} %slice.205), channel_id=1, source_target_pairs={{0,8},{8,16},{16,24},{1,9},{9,17},{17,25},{2,10},{10,18},{18,26},{... | collective-permute-start | bytes 6152 | tf_op jit(solution)/shard_map/ppermute | solution.py:26
  87.9 6.6 %copy-start.60 = (f32[1,512]{1,0:T(1,128)S(1)}, f32[1,512]{1,0:T(1,128)}, u32[]{:S(2)}) copy-start(f32[1,512]{1,0:T(1,128)} %copy-done.59) | copy-start | bytes 6148
  91.0 14.8 %all-to-all-start.1 = ((bf16[384,2,4,128]{3,0,1,2:T(8,128)(2,1)}), bf16[384,2,4,128]{3,0,1,2:T(8,128)(2,1)S(1)}, u32[]{:S(2)}, u32[]{:S(2)}) async-start(bf16[384,2,4,128]{3,0,1,2:T(8,128)(2,1)} %copy.137), calls=%async_computation.1 | async-start | bytes 1572864 | tf_op jit(solution)/shard_map/all_to_all | solution.py:648
  106.7 18.4 %all-to-all-start = ((bf16[1152,1,4,128]{3,0,1,2:T(8,128)(2,1)}), bf16[1152,1,4,128]{3,0,1,2:T(8,128)(2,1)S(1)}, u32[]{:S(2)}, u32[]{:S(2)}) async-start(bf16[1152,1,4,128]{3,0,1,2:T(8,128)(2,1)} %copy.135), calls=%async_computation | async-start | bytes 2359296 | tf_op jit(solution)/shard_map/all_to_all | solution.py:641
  156.6 19.2 %all-to-all-start.2 = ((bf16[4,2,73728]{2,1,0:T(2,128)(2,1)}), bf16[4,2,73728]{2,1,0:T(2,128)(2,1)}, u32[]{:S(2)}, u32[]{:S(2)}) async-start(bf16[4,2,73728]{2,1,0:T(2,128)(2,1)} %reshape.340), calls=%async_computation.2 | async-start | bytes 2359296 | tf_op jit(solution)/shard_map/all_to_all | solution.py:663
  184.6 10.4 %copy-start.39 = (f32[1152]{0:T(1024)}, f32[1152]{0:T(1024)S(1)}, u32[]{:S(2)}) copy-start(f32[1152]{0:T(1024)S(1)} %broadcast_multiply_fusion.4) | copy-start | bytes 13828
  184.9 10.1 %copy-start.41 = (f32[1152]{0:T(1024)}, f32[1152]{0:T(1024)S(1)}, u32[]{:S(2)}) copy-start(f32[1152]{0:T(1024)S(1)} %add_rsqrt_fusion) | copy-start | bytes 13828
  201.7 9.4 %copy-start.5 = (bf16[1,1152,512]{1,2,0:T(8,128)(2,1)S(1)}, bf16[1,1152,512]{1,2,0:T(8,128)(2,1)}, u32[]{:S(2)}) copy-start(bf16[1,1152,512]{1,2,0:T(8,128)(2,1)} %copy.142) | copy-start | bytes 3538948
  201.7 9.4 %copy-start.51 = (f32[1152]{0:T(1024)S(1)}, f32[1152]{0:T(1024)}, u32[]{:S(2)}) copy-start(f32[1152]{0:T(1024)} %fusion.71) | copy-start | bytes 13828
  201.7 9.4 %copy-start.70 = (bf16[2,2,4,2,64,512]{5,4,3,2,1,0:T(8,128)(2,1)S(1)}, bf16[2,2,4,2,64,512]{5,4,3,2,1,0:T(8,128)(2,1)}, u32[]{:S(2)}) copy-start(bf16[2,2,4,2,64,512]{5,4,3,2,1,0:T(8,128)(2,1)} %get-tuple-element.40) | copy-start | bytes 6291460
  201.7 9.5 %copy-start.71 = (f32[1152,2048]{1,0:T(8,128)S(1)}, f32[1152,2048]{1,0:T(8,128)}, u32[]{:S(2)}) copy-start(f32[1152,2048]{1,0:T(8,128)} %get-tuple-element.258) | copy-start | bytes 28311556
  247.0 19.0 %all-to-all-start.3 = ((bf16[1152,1,4,128]{3,0,1,2:T(8,128)(2,1)}), bf16[1152,1,4,128]{3,0,1,2:T(8,128)(2,1)}, u32[]{:S(2)}, u32[]{:S(2)}) async-start(bf16[1152,1,4,128]{3,0,1,2:T(8,128)(2,1)} %copy.144), calls=%async_computation.3 | async-start | bytes 2359296 | tf_op jit(solution)/shard_map/all_to_all | solution.py:690
  297.5 11.1 %copy-start.7 = (bf16[1,1152,512]{1,2,0:T(8,128)(2,1)S(1)}, bf16[1,1152,512]{1,2,0:T(8,128)(2,1)}, u32[]{:S(2)}) copy-start(bf16[1,1152,512]{1,2,0:T(8,128)(2,1)} %copy.142) | copy-start | bytes 3538948
  297.5 11.1 %copy-start.53 = (f32[1152]{0:T(1024)S(1)}, f32[1152]{0:T(1024)}, u32[]{:S(2)}) copy-start(f32[1152]{0:T(1024)} %fusion.71) | copy-start | bytes 13828
  305.1 15.0 %all-to-all-start.5 = ((bf16[1536,2,1,128]{3,1,2,0:T(2,128)(2,1)}), bf16[1536,2,1,128]{3,1,2,0:T(2,128)(2,1)S(1)}, u32[]{:S(2)}, u32[]{:S(2)}) async-start(bf16[1536,2,1,128]{3,1,2,0:T(2,128)(2,1)} %copy.147), calls=%async_computation.5 | async-start | bytes 1572864 | tf_op jit(solution)/shard_map/all_to_all | solution.py:713
  320.1 28.7 %all-to-all-start.4 = ((bf16[4,2,73728]{2,1,0:T(2,128)(2,1)}), bf16[4,2,73728]{2,1,0:T(2,128)(2,1)}, u32[]{:S(2)}, u32[]{:S(2)}) async-start(bf16[4,2,73728]{2,1,0:T(2,128)(2,1)} %reshape.342), calls=%async_computation.4 | async-start | bytes 2359296 | tf_op jit(solution)/shard_map/all_to_all | solution.py:706
  336.5 22.2 %collective-permute-start.1 = (f32[2,512]{0,1:T(8,128)}, f32[2,512]{0,1:T(8,128)}, u32[]{:S(2)}, u32[]{:S(2)}) collective-permute-start(f32[2,512]{0,1:T(8,128)} %copy.170), channel_id=1, source_target_pairs={{8,0},{16,8},{24,16},{9,1},{17,9},{25,17},{10,2},{18,10},{26,18},{... | collective-permute-start | bytes 12296 | tf_op jit(solution)/shard_map/ppermute | solution.py:26
  385.2 69.4 %copy-start.29 = (f32[64,512]{1,0:T(8,128)S(1)}, f32[64,512]{1,0:T(8,128)}, u32[]{:S(2)}) copy-start(f32[64,512]{1,0:T(8,128)} %wd.1) | copy-start | bytes 393220
  385.2 69.4 %copy-start.33 = (f32[64,512]{1,0:T(8,128)S(1)}, f32[64,512]{1,0:T(8,128)}, u32[]{:S(2)}) copy-start(f32[64,512]{1,0:T(8,128)} %param.40) | copy-start | bytes 393220
  385.2 69.4 %copy-start.34 = (f32[64,512]{1,0:T(8,128)S(1)}, f32[64,512]{1,0:T(8,128)}, u32[]{:S(2)}) copy-start(f32[64,512]{1,0:T(8,128)} %param.34) | copy-start | bytes 393220
  385.2 71.1 %copy-start.45 = (f32[9,16]{1,0:T(8,128)S(1)}, f32[9,16]{1,0:T(8,128)}, u32[]{:S(2)}) copy-start(f32[9,16]{1,0:T(8,128)} %param.29) | copy-start | bytes 1732
  385.2 71.1 %copy-start.63 = (f32[9,16]{1,0:T(8,128)S(1)}, f32[9,16]{1,0:T(8,128)}, u32[]{:S(2)}) copy-start(f32[9,16]{1,0:T(8,128)} %param.41) | copy-start | bytes 1732
  385.2 71.1 %copy-start.64 = (f32[9,16]{1,0:T(8,128)S(1)}, f32[9,16]{1,0:T(8,128)}, u32[]{:S(2)}) copy-start(f32[9,16]{1,0:T(8,128)} %param.35) | copy-start | bytes 1732
  385.2 72.5 %copy-start.37 = (f32[16,512]{1,0:T(8,128)S(1)}, f32[16,512]{1,0:T(8,128)}, u32[]{:S(2)}) copy-start(f32[16,512]{1,0:T(8,128)} %wq.1) | copy-start | bytes 98308
  385.2 72.5 %copy-start.38 = (f32[16,512]{1,0:T(8,128)S(1)}, f32[16,512]{1,0:T(8,128)}, u32[]{:S(2)}) copy-start(f32[16,512]{1,0:T(8,128)} %wo.1) | copy-start | bytes 98308
  385.2 72.5 %copy-start.47 = (f32[16,512]{1,0:T(8,128)S(1)}, f32[16,512]{1,0:T(8,128)}, u32[]{:S(2)}) copy-start(f32[16,512]{1,0:T(8,128)} %param.38) | copy-start | bytes 98308
  385.2 72.5 %copy-start.48 = (f32[16,512]{1,0:T(8,128)S(1)}, f32[16,512]{1,0:T(8,128)}, u32[]{:S(2)}) copy-start(f32[16,512]{1,0:T(8,128)} %param.32) | copy-start | bytes 98308
  385.2 72.5 %copy-start.49 = (f32[16,512]{1,0:T(8,128)S(1)}, f32[16,512]{1,0:T(8,128)}, u32[]{:S(2)}) copy-start(f32[16,512]{1,0:T(8,128)} %param.36) | copy-start | bytes 98308
  385.3 72.5 %copy-start.50 = (f32[16,512]{1,0:T(8,128)S(1)}, f32[16,512]{1,0:T(8,128)}, u32[]{:S(2)}) copy-start(f32[16,512]{1,0:T(8,128)} %param.30) | copy-start | bytes 98308
  453.4 6.7 %copy-start.30 = (f32[16,2048]{1,0:T(8,128)S(1)}, f32[16,2048]{1,0:T(8,128)}, u32[]{:S(2)}) copy-start(f32[16,2048]{1,0:T(8,128)} %wu.1) | copy-start | bytes 393220
  453.4 6.7 %copy-start.35 = (f32[16,2048]{1,0:T(8,128)S(1)}, f32[16,2048]{1,0:T(8,128)}, u32[]{:S(2)}) copy-start(f32[16,2048]{1,0:T(8,128)} %param.39) | copy-start | bytes 393220
  453.4 6.7 %copy-start.36 = (f32[16,2048]{1,0:T(8,128)S(1)}, f32[16,2048]{1,0:T(8,128)}, u32[]{:S(2)}) copy-start(f32[16,2048]{1,0:T(8,128)} %param.33) | copy-start | bytes 393220
  (48 other events, 132.1 us)
